TPU v7x, 256 devices: a whole 4x4x8 slice. The times are simulated.
256 devices in a mesh: slab: 16 (over z, core), cell: 16 (over x, y).
Axes of the slice: x: 4, y: 4, z: 8, core: 2. Of those that a mesh axis runs over, the one named last changes fastest.
Arguments:
- centers: float32 [3, 16384], P(None, ('slab', 'cell')), may hold values from -0.8 to 0.8
- offsets: float32 [3, 16384, 312], P(None, ('slab', 'cell')), may hold values from -0.5 to 0.5
- forces: float32 [3, 16384, 312], P(None, ('slab', 'cell')), may hold values from -6 to 6
- upsample: float32 [312, 1248], replicated, may hold values from -0.3125 to 0.3125
- translate: float32 [3, 165, 165], replicated, may hold values from -0.5 to 0.5
- owner_cell: int32 [256, 16, 2], P(('slab', 'cell')), may hold values from 0 to 63, as said below
- peer_cell: int32 [256, 16, 2], P(('slab', 'cell')), may hold values from 0 to 63, as said below
- live: int32 [256, 16, 2], P(('slab', 'cell')), may hold values 0 or 1
Outputs:
- velocity: float32 [3, 16384, 312], P(None, ('slab', 'cell'))
Inputs may be any that keep to these rules, and one draw needn't show every extreme that they name: `owner_cell`: every cell takes part in at most one pair slot of all devices, as owner or as partner. `peer_cell`: every cell takes part in at most one pair slot of all devices, as owner or as partner.
All inputs are finite; a program needn't handle non-finite values. No bound on the sum of `live` on one device may be relied on, other than what follows from the above.
Results may differ from a plain program's by a relative error of at most 0.00019.
Values sent between devices are 32-bit elements; how exact they have to be, the bound alone decides.
A program may use at most 64 MiB of HBM per device.

v0:
```python
import functools
import math

import jax
import jax.numpy as jnp
from jax import lax
from jax.experimental import pallas as pl
from jax.experimental.pallas import tpu as pltpu
from jax.sharding import PartitionSpec as P

DEGREE = 8
NT = 165
SOFTEN = 0.0025
STRETCH = 20.0
LANES = 384
UP_LANES = 1280
f32 = jnp.float32
bf16 = jnp.bfloat16
MESH = pl.DeviceIdType.MESH
highest = lax.Precision.HIGHEST
NT_DIMS = (((1,), (1,)), ((), ()))


def split3(x):
    first = x.astype(bf16).astype(f32)
    rest = x - first
    second = rest.astype(bf16).astype(f32)
    third = (rest - second).astype(bf16).astype(f32)
    return first, second, third


def exchange_kernel(
    owner, peer, live, centers, offsets, forces, translate,
    got_a, got_b, got_meta, block, points, local,
    send_a, send_b, send_meta, meta_here, mom_out, mom_in, total, beside, padded, acc,
    send_sems, recv_sems, side_send, side_recv, here_sem,
):
    n_cell = lax.axis_size("cell")
    n_slab = lax.axis_size("slab")
    me = lax.axis_index("cell")
    slab = lax.axis_index("slab")
    above = lax.rem(slab + 1, n_slab)
    below = lax.rem(slab + n_slab - 1, n_slab)
    cells, count = offsets.shape[1], offsets.shape[2]

    barrier = pltpu.get_barrier_semaphore()

    def greet(j, carry):
        to = lax.rem(me + j, n_cell)
        pl.semaphore_signal(barrier, inc=1, device_id={"cell": to}, device_id_type=MESH)
        return carry

    lax.fori_loop(1, n_cell, greet, 0)
    for side in (above, below):
        pl.semaphore_signal(barrier, inc=1, device_id={"slab": side}, device_id_type=MESH)

    lane = lax.broadcasted_iota(jnp.int32, (cells, LANES), 1)
    diag = lax.broadcasted_iota(jnp.int32, (cells, cells), 0) == lax.broadcasted_iota(jnp.int32, (cells, cells), 1)
    block[...] = jnp.zeros_like(block)
    for d in range(3):
        column = jnp.sum(jnp.where(diag, centers[d : d + 1, :], 0.0), axis=1, keepdims=True)
        padded[d, :, 0:count] = offsets[d]
        padded[3 + d, :, 0:count] = forces[d]
        shift = jnp.where(lane < count, padded[d], jnp.where(lane == count, column, 0.0))
        force = jnp.where(lane < count, padded[3 + d], 0.0)
        block[:, d, :] = shift
        block[:, 4 + d, :] = force
        padded[3 + d] = force
        points[d] = jnp.where(lane < count, shift + column, 0.0)

    small = lax.broadcasted_iota(jnp.int32, (8, 128), 1)
    for q in range(n_cell):
        for k in range(2):
            send_a[q, k] = block[owner[0, q, k]]
        row = jnp.where(small == 0, peer[0, q, 0], peer[0, q, 1])
        row = jnp.where(small == 2, live[0, q, 0], row)
        send_meta[q] = jnp.where(small == 3, live[0, q, 1], row)

    pl.semaphore_wait(barrier, n_cell + 1)

    def copy(kind, source, target, j):
        to = lax.rem(me + j, n_cell)
        return pltpu.make_async_remote_copy(
            src_ref=source if kind == 3 else source.at[to],
            dst_ref=target.at[me],
            send_sem=send_sems.at[kind, j],
            recv_sem=recv_sems.at[kind, j],
            device_id={"cell": to},
            device_id_type=MESH,
        )

    def each(action):
        def step(j, carry):
            action(j)
            return carry

        lax.fori_loop(1, n_cell, step, 0)

    def arrival(kind, source, target, j):
        origin = lax.rem(me + n_cell - j, n_cell)
        return pltpu.make_async_remote_copy(
            src_ref=source if kind == 3 else source.at[origin],
            dst_ref=target.at[origin],
            send_sem=send_sems.at[kind, j],
            recv_sem=recv_sems.at[kind, j],
            device_id={"cell": origin},
            device_id_type=MESH,
        )

    each(lambda j: copy(0, send_meta, got_meta, j).start())
    each(lambda j: copy(1, send_a, got_a, j).start())
    got_meta[me] = send_meta[me]
    got_a[me] = send_a[me]
    each(lambda j: arrival(0, send_meta, got_meta, j).wait_recv())
    fetch = pltpu.make_async_copy(got_meta, meta_here, here_sem)
    fetch.start()
    fetch.wait()
    for q in range(n_cell):
        for k in range(2):
            send_b[q, k] = block[meta_here[q, 0, k]]
    each(lambda j: copy(2, send_b, got_b, j).start())
    got_b[me] = send_b[me]

    acc[...] = jnp.zeros_like(acc)

    def moment_rows(i, carry):
        rows = pl.ds(pl.multiple_of(i * 8, 8), 8)
        x, y, z = points[0, rows], points[1, rows], points[2, rows]
        force = [padded[3 + d, rows] for d in range(3)]
        t = 0
        power_x = jnp.ones_like(x)
        for a in range(DEGREE + 1):
            power_y = power_x
            for b in range(DEGREE + 1 - a):
                term = power_y
                for c in range(DEGREE + 1 - a - b):
                    for d in range(3):
                        v = term * force[d]
                        acc[d, t] += v[:, 0:128] + v[:, 128:256] + v[:, 256:384]
                    t += 1
                    if c < DEGREE - a - b:
                        term = term * z
                if b < DEGREE - a:
                    power_y = power_y * y
            if a < DEGREE:
                power_x = power_x * x
        return carry

    lax.fori_loop(0, cells // 8, moment_rows, 0)
    scale = 1.0 / math.sqrt(cells * n_cell * count)
    terms = acc.shape[1]
    sub = lax.broadcasted_iota(jnp.int32, (8, terms), 0)
    moments = jnp.zeros((8, terms), f32)
    for d in range(3):
        part = jnp.sum(acc[d], axis=1)
        row = lax.dot_general(jnp.ones((8, 128), f32), part, NT_DIMS, precision=highest, preferred_element_type=f32)
        moments = jnp.where(sub == d, row * scale, moments)
    mom_out[...] = jnp.zeros_like(mom_out)
    mom_out[:, 0:terms] = moments
    each(lambda j: copy(3, mom_out, mom_in, j).start())
    mom_in[me] = mom_out[...]
    each(lambda j: arrival(3, mom_out, mom_in, j).wait_recv())
    gathered = mom_in[0]
    for q in range(1, n_cell):
        gathered = gathered + mom_in[q]
    total[...] = gathered

    def side_copy(which, to):
        return pltpu.make_async_remote_copy(
            src_ref=total,
            dst_ref=beside.at[which],
            send_sem=side_send.at[which],
            recv_sem=side_recv.at[which],
            device_id={"slab": to},
            device_id_type=MESH,
        )

    up_copy, down_copy = side_copy(0, above), side_copy(1, below)
    up_copy.start()
    down_copy.start()
    up_copy.wait()
    down_copy.wait()
    lower = jnp.where(slab == 0, 0.0, beside[0])
    upper = jnp.where(slab == n_slab - 1, 0.0, beside[1])
    coef = jnp.zeros((8, NT), f32)
    for k, source in enumerate((total[...], lower, upper)):
        coef = coef + lax.dot_general(
            source[:, 0:NT], translate[k], NT_DIMS, precision=highest, preferred_element_type=f32
        )
    local[...] = jnp.zeros_like(local)
    local[:, 0:NT] = coef

    each(lambda j: arrival(1, send_a, got_a, j).wait_recv())
    each(lambda j: arrival(2, send_b, got_b, j).wait_recv())
    each(lambda j: copy(0, send_meta, got_meta, j).wait_send())
    each(lambda j: copy(1, send_a, got_a, j).wait_send())
    each(lambda j: copy(2, send_b, got_b, j).wait_send())
    each(lambda j: copy(3, mom_out, mom_in, j).wait_send())


def field_kernel(
    meta, owner, live, local, block, got_a, got_b, points, upsample,
    out,
    cell_list, packed, spread, up_high, up_low, left, right, table, columns,
):
    cells, count, up_count = out.shape[1], out.shape[2], upsample.shape[1]
    n_cell = got_a.shape[0]

    def far_rows(i, carry):
        rows = pl.ds(pl.multiple_of(i * 16, 16), 16)
        x, y, z = points[0, rows], points[1, rows], points[2, rows]
        index = {}
        t = 0
        for a in range(DEGREE + 1):
            for b in range(DEGREE + 1 - a):
                for c in range(DEGREE + 1 - a - b):
                    index[a, b, c] = t
                    t += 1
        for d in range(3):
            in_x = None
            for a in range(DEGREE, -1, -1):
                in_y = None
                for b in range(DEGREE - a, -1, -1):
                    in_z = None
                    for c in range(DEGREE - a - b, -1, -1):
                        value = local[d, index[a, b, c]]
                        in_z = value if in_z is None else in_z * z + value
                    in_y = in_z if in_y is None else in_y * y + in_z
                in_x = in_y if in_x is None else in_x * x + in_y
            out[d, rows, :] = in_x[:, 0:count]
        return carry

    lax.fori_loop(0, cells // 16, far_rows, 0)

    def list_slot(s, n):
        q, k = s // 2, lax.rem(s, 2)
        flag, cell = live[0, q, k], owner[0, q, k]

        @pl.when(flag > 0)
        def _():
            cell_list[n] = cell
            packed[n] = got_b[q, k]

        n = n + jnp.where(flag > 0, 1, 0)
        flag_in, cell_in = meta[q, 0, 2 + k], meta[q, 0, k]

        @pl.when(flag_in > 0)
        def _():
            cell_list[n] = cell_in
            packed[n] = got_a[q, k]

        return n + jnp.where(flag_in > 0, 1, 0)

    units = lax.fori_loop(0, 2 * n_cell, list_slot, jnp.int32(0))

    up_high[...] = jnp.zeros_like(up_high)
    up_low[...] = jnp.zeros_like(up_low)
    whole = upsample[...]
    high = whole.astype(bf16)
    up_high[:, 0:up_count] = high
    up_low[:, 0:up_count] = (whole - high.astype(f32)).astype(bf16)

    def spread_units(i, carry):
        rows = pl.ds(i * 16, 16)
        data = packed[rows].reshape(128, LANES)[:, 0:count]
        first = data.astype(bf16)
        second = (data - first.astype(f32)).astype(bf16)
        result = (
            jnp.dot(first, up_high[...], preferred_element_type=f32)
            + jnp.dot(second, up_high[...], preferred_element_type=f32)
            + jnp.dot(first, up_low[...], preferred_element_type=f32)
        )
        spread[rows] = result.reshape(16, 8, UP_LANES)
        return carry

    lax.fori_loop(0, (units + 15) // 16, spread_units, 0)

    def build(u, carry):
        cell = cell_list[u]
        target = block[cell]
        row = lax.broadcasted_iota(jnp.int32, (8, UP_LANES), 0)
        between = packed[u][:, count : count + 1] - target[:, count : count + 1]
        z = jnp.where(row < 3, STRETCH * (spread[u] + between), spread[u])
        table[u] = z
        square = jnp.sum(jnp.where(row < 3, z * z, 0.0), axis=0, keepdims=True) + 1.0
        aligned = jnp.concatenate([z[4:8], z[0:4]], axis=0)
        product = jnp.sum(jnp.where(row < 3, z * aligned, 0.0), axis=0, keepdims=True)
        feature = jnp.where(row < 3, -2.0 * z, jnp.where(row == 3, square, jnp.where(row == 7, -product, z)))
        f1, f2, f3 = split3(feature)
        constant = jnp.where(row < 3, 1.0, 0.0)
        for k, pair in enumerate(((f1, f2), (f1, f3), (f2, f1), (constant, jnp.zeros_like(constant)))):
            right[u, 16 * k : 16 * k + 16] = jnp.concatenate(pair, axis=0).astype(bf16)

        small = lax.broadcasted_iota(jnp.int32, (8, LANES), 0)
        y = jnp.where(small < 3, STRETCH * target, 0.0)
        yy = jnp.sum(y * y, axis=0, keepdims=True)
        y1, y2, y3 = split3(y)
        s1, s2, s3 = split3(yy)
        one = jnp.where(small == 3, 1.0, y1)
        squares = jnp.where(small == 0, s1, jnp.where(small == 1, s2, jnp.where(small == 2, s3, 0.0)))
        zero = jnp.zeros_like(y)
        order = [one, one, y2, one, y2, y3]
        lower = [jnp.concatenate([v[4:8], v[0:4]], axis=0) for v in order]
        for k, rows in enumerate((order + [squares, zero], lower + [zero, zero])):
            turned = jnp.transpose(jnp.concatenate(rows, axis=0))
            left[u, k] = turned[0:count].astype(bf16)
        return carry

    lax.fori_loop(0, units, build, 0)

    columns[...] = jnp.zeros_like(columns)
    step = 40

    def one_unit(u, carry):
        cell = cell_list[u]
        for begin in range(0, count, step):
            size = min(step, count - begin)
            near = [jnp.zeros((size, 128), f32) for _ in range(4)]
            left_s = left[u, 0, begin : begin + size]
            left_p = left[u, 1, begin : begin + size]
            for c in range(UP_LANES // 128):
                lanes = slice(c * 128, c * 128 + 128)
                feature = right[u, :, lanes]
                inverse = lax.rsqrt(jnp.dot(left_s, feature, preferred_element_type=f32))
                projected = jnp.dot(left_p, feature, preferred_element_type=f32)
                cube = inverse * inverse * inverse
                along = inverse + cube
                across = cube * projected
                for d in range(3):
                    near[d] = near[d] + (
                        along * table[u, 4 + d : 5 + d, lanes] - across * table[u, d : d + 1, lanes]
                    )
                near[3] = near[3] + across
            for d in range(4):
                columns[begin : begin + size, d : d + 1] = jnp.sum(near[d], axis=1, keepdims=True)
        sums = jnp.transpose(columns[...])[0:8]
        small = lax.broadcasted_iota(jnp.int32, (8, LANES), 0)
        y = jnp.where(small < 3, STRETCH * block[cell], 0.0)
        velocity = (sums + y * sums[3:4]) * (STRETCH / up_count)
        for d in range(3):
            out[d, pl.ds(cell, 1), :] += velocity[d : d + 1, 0:count]
        return carry

    lax.fori_loop(0, units, one_unit, 0)


def on_device(centers, offsets, forces, upsample, translate, owner_cell, peer_cell, live):
    cells, count = offsets.shape[1], offsets.shape[2]
    n_cell = owner_cell.shape[1]
    vmem = pl.BlockSpec(memory_space=pltpu.VMEM)
    smem = pl.BlockSpec(memory_space=pltpu.SMEM)
    slots = (n_cell, 2, 8, LANES)
    got_a, got_b, got_meta, block, points, local = pl.pallas_call(
        exchange_kernel,
        out_shape=(
            jax.ShapeDtypeStruct(slots, f32),
            jax.ShapeDtypeStruct(slots, f32),
            jax.ShapeDtypeStruct((n_cell, 8, 128), jnp.int32),
            jax.ShapeDtypeStruct((cells, 8, LANES), f32),
            jax.ShapeDtypeStruct((3, cells, LANES), f32),
            jax.ShapeDtypeStruct((8, 256), f32),
        ),
        in_specs=[smem] * 3 + [vmem] * 4,
        out_specs=(vmem,) * 6,
        scratch_shapes=[
            pltpu.VMEM(slots, f32),
            pltpu.VMEM(slots, f32),
            pltpu.VMEM((n_cell, 8, 128), jnp.int32),
            pltpu.SMEM((n_cell, 8, 128), jnp.int32),
            pltpu.VMEM((8, 256), f32),
            pltpu.VMEM((n_cell, 8, 256), f32),
            pltpu.VMEM((8, 256), f32),
            pltpu.VMEM((2, 8, 256), f32),
            pltpu.VMEM((6, cells, LANES), f32),
            pltpu.VMEM((3, 168, 8, 128), f32),
            pltpu.SemaphoreType.DMA((4, n_cell)),
            pltpu.SemaphoreType.DMA((4, n_cell)),
            pltpu.SemaphoreType.DMA((2,)),
            pltpu.SemaphoreType.DMA((2,)),
            pltpu.SemaphoreType.DMA,
        ],
        compiler_params=pltpu.CompilerParams(
            collective_id=0, has_side_effects=True, vmem_limit_bytes=32 * 1024 * 1024
        ),
        name="exchange",
    )(owner_cell, peer_cell, live, centers, offsets, forces, translate)
    return pl.pallas_call(
        field_kernel,
        out_shape=jax.ShapeDtypeStruct((3, cells, count), f32),
        in_specs=[smem] * 4 + [vmem] * 5,
        out_specs=vmem,
        scratch_shapes=[
            pltpu.SMEM((cells,), jnp.int32),
            pltpu.VMEM((cells, 8, LANES), f32),
            pltpu.VMEM((cells, 8, UP_LANES), f32),
            pltpu.VMEM((count, UP_LANES), bf16),
            pltpu.VMEM((count, UP_LANES), bf16),
            pltpu.VMEM((cells, 2, count, 64), bf16),
            pltpu.VMEM((cells, 64, UP_LANES), bf16),
            pltpu.VMEM((cells, 8, UP_LANES), f32),
            pltpu.VMEM((LANES, 128), f32),
        ],
        compiler_params=pltpu.CompilerParams(vmem_limit_bytes=50 * 1024 * 1024),
        name="field",
    )(got_meta, owner_cell, live, local, block, got_a, got_b, points, upsample)


def solution(mesh):
    return jax.shard_map(
        on_device,
        mesh=mesh,
        in_specs=(
            P(None, ("slab", "cell")),
            P(None, ("slab", "cell"), None),
            P(None, ("slab", "cell"), None),
            P(),
            P(),
            P(("slab", "cell"), None, None),
            P(("slab", "cell"), None, None),
            P(("slab", "cell"), None, None),
        ),
        out_specs=P(None, ("slab", "cell"), None),
        check_vma=False,
    )
```

profile of v0, /device:TPU:129, one launch (start us, length us, event | category | flops | bytes accessed | tf_op | source)
XLA Modules:
  0.0 108.7 jit_solution(7376737627637892474)
XLA Ops:
  0.0 0.8 copy.9.owner
  0.8 0.8 copy.11.live
  1.5 0.8 copy.10.peer
  2.3 0.0 copy-start.1
  2.3 1.0 copy-done.1
  3.3 0.0 copy-start.2
  3.3 1.0 copy-done.2
  4.3 0.0 copy-start.3
  4.3 1.0 copy-done.3
  5.2 0.0 copy-start.4
  5.2 0.7 copy-done.4
  5.9 29.1 %exchange.1 = (f32[16,2,8,384]{3,2,1,0:T(8,128)S(1)}, f32[16,2,8,384]{3,2,1,0:T(8,128)S(1)}, s32[16,8,128]{2,1,0:T(8,128)S(1)}, f32[64,8,384]{2,1,0:T(8,128)S(1)...) custom-call(s32[1,16,2]{2,1,0:T(8,128)S(1)} %copy.9.owner, s32[1,16,2]{2,1,0:T(8,128)S(1)} %copy.10.peer, ...), custom_call_target="tpu_custom_call" | custom-call | tf_op jit(solution)/shard_map/exchange/pallas_call | solution.py:353
  35.0 0.0 copy-start
  35.1 1.4 %copy-done = f32[312,1248]{1,0:T(8,128)S(1)} copy-done((f32[312,1248]{1,0:T(8,128)S(1)}, f32[312,1248]{1,0:T(8,128)}, u32[]{:S(2)}) %copy-start) | copy-done | bytes 1557528
  36.5 72.3 %field.1 = f32[3,64,312]{2,1,0:T(8,128)} custom-call(s32[16,8,128]{2,1,0:T(8,128)S(1)} %get-tuple-element.11.meta, s32[1,16,2]{2,1,0:T(8,128)S(1)} %copy.9.owner, s32[1,16,2]{2,1,0:T(8,128)S(1)} %copy.11.live, f32[8,256]{1,0:T(8,128)S(1)} %get-tuple-element.12.local, f32[64,8,384]{2,1,0:T(8,128)S(1)} %get-tuple-element.13.block, ...), custom_call_target="tpu_custom_call" | custom-call | tf_op jit(solution)/shard_map/field/pallas_call | solution.py:387
Async XLA Ops:
  2.3 1.0 copy-start.1
  3.3 1.0 copy-start.2
  4.3 1.0 copy-start.3
  5.2 0.7 copy-start.4
  35.0 1.4 %copy-start = (f32[312,1248]{1,0:T(8,128)S(1)}, f32[312,1248]{1,0:T(8,128)}, u32[]{:S(2)}) copy-start(f32[312,1248]{1,0:T(8,128)} %upsample.1) | copy-start | bytes 4672516
where the time goes:
time: 109 us
  Pallas kernels  101 us (93%)
  local copies, waits for them, and re-layouts  7.32 us (7%)
    pallas_call x1, Pallas kernels, on_device(): pl.pallas_call(field_kernel, out_shape=jax.ShapeDtypeStruct((3, cells, co...  72.3 us
    pallas_call x1, Pallas kernels, on_device(): pl.pallas_call(exchange_kernel, out_shape=(jax.ShapeDtypeStruct(slots, f3...  29.1 us
    unnamed x13, local copies, waits for them, and re-layouts  7.32 us

commit v1 on v0

--- a/solution.py
+++ b/solution.py
@@ -30,10 +30,11 @@
 
 
 def exchange_kernel(
-    owner, peer, live, centers, offsets, forces, translate,
-    got_a, got_b, got_meta, block, points, local,
-    send_a, send_b, send_meta, meta_here, mom_out, mom_in, total, beside, padded, acc,
-    send_sems, recv_sems, side_send, side_recv, here_sem,
+    owner, peer, live, centers_hbm, offsets_hbm, forces_hbm, translate_hbm,
+    got_a, got_b, meta, block, points, local,
+    centers, offsets, forces, translate, sent, send_a, send_b, send_meta, got_meta, merged, meta_here,
+    mom_out, mom_in, total, beside, padded, acc,
+    send_sems, recv_sems, side_send, side_recv, here_sems,
 ):
     n_cell = lax.axis_size("cell")
     n_slab = lax.axis_size("slab")
@@ -44,6 +45,10 @@
     cells, count = offsets.shape[1], offsets.shape[2]
 
     barrier = pltpu.get_barrier_semaphore()
+    pairs = ((centers_hbm, centers), (offsets_hbm, offsets), (forces_hbm, forces), (translate_hbm, translate))
+    loads = [pltpu.make_async_copy(source, target, here_sems.at[k]) for k, (source, target) in enumerate(pairs)]
+    for load in loads:
+        load.start()
 
     def greet(j, carry):
         to = lax.rem(me + j, n_cell)
@@ -54,71 +59,90 @@
     for side in (above, below):
         pl.semaphore_signal(barrier, inc=1, device_id={"slab": side}, device_id_type=MESH)
 
+    small = lax.broadcasted_iota(jnp.int32, (8, 128), 1) - 4 * me
+    for q in range(n_cell):
+        row = jnp.zeros((8, 128), jnp.int32)
+        for k in range(2):
+            row = jnp.where(small == k, peer[0, k, q], row)
+            row = jnp.where(small == 2 + k, live[0, k, q], row)
+        send_meta[q] = row
+
+    for load in loads[:3]:
+        load.wait()
+
     lane = lax.broadcasted_iota(jnp.int32, (cells, LANES), 1)
+    tail_lane = lax.broadcasted_iota(jnp.int32, (cells, 128), 1)
     diag = lax.broadcasted_iota(jnp.int32, (cells, cells), 0) == lax.broadcasted_iota(jnp.int32, (cells, cells), 1)
     block[...] = jnp.zeros_like(block)
+    tails = []
+    middle = jnp.zeros((cells, 128), f32)
     for d in range(3):
         column = jnp.sum(jnp.where(diag, centers[d : d + 1, :], 0.0), axis=1, keepdims=True)
         padded[d, :, 0:count] = offsets[d]
         padded[3 + d, :, 0:count] = forces[d]
-        shift = jnp.where(lane < count, padded[d], jnp.where(lane == count, column, 0.0))
+        offset = jnp.where(lane < count, padded[d], 0.0)
         force = jnp.where(lane < count, padded[3 + d], 0.0)
-        block[:, d, :] = shift
+        block[:, d, :] = jnp.where(lane == count, column, offset)
         block[:, 4 + d, :] = force
+        sent[:, d, :] = offset[:, 0:256]
+        sent[:, 4 + d, :] = force[:, 0:256]
         padded[3 + d] = force
-        points[d] = jnp.where(lane < count, shift + column, 0.0)
-
-    small = lax.broadcasted_iota(jnp.int32, (8, 128), 1)
+        points[d] = jnp.where(lane < count, offset + column, 0.0)
+        tails.append((offset[:, 256:384], force[:, 256:384]))
+        middle = jnp.where(tail_lane == 64 + d, column, middle)
+    for k in range(2):
+        sent[:, 3 + 4 * k, 0:128] = tails[0][k] + pltpu.roll(tails[1][k], 64, 1)
+        sent[:, 3 + 4 * k, 128:256] = tails[2][k] + middle
+
     for q in range(n_cell):
         for k in range(2):
-            send_a[q, k] = block[owner[0, q, k]]
-        row = jnp.where(small == 0, peer[0, q, 0], peer[0, q, 1])
-        row = jnp.where(small == 2, live[0, q, 0], row)
-        send_meta[q] = jnp.where(small == 3, live[0, q, 1], row)
+            send_a[q, k] = sent[owner[0, k, q]]
 
     pl.semaphore_wait(barrier, n_cell + 1)
 
-    def copy(kind, source, target, j):
-        to = lax.rem(me + j, n_cell)
+    def send(kind, source, target):
+        def step(j, carry):
+            to = lax.rem(me + j, n_cell)
+            pltpu.make_async_remote_copy(
+                src_ref=source if kind == 3 else source.at[to],
+                dst_ref=target.at[me],
+                send_sem=send_sems.at[kind],
+                recv_sem=recv_sems.at[kind],
+                device_id={"cell": to},
+                device_id_type=MESH,
+            ).start()
+            return carry
+
+        lax.fori_loop(1, n_cell, step, 0)
+
+    def every(kind, target):
+        part = target.at[pl.ds(0, n_cell - 1)]
         return pltpu.make_async_remote_copy(
-            src_ref=source if kind == 3 else source.at[to],
-            dst_ref=target.at[me],
-            send_sem=send_sems.at[kind, j],
-            recv_sem=recv_sems.at[kind, j],
-            device_id={"cell": to},
+            src_ref=part,
+            dst_ref=part,
+            send_sem=send_sems.at[kind],
+            recv_sem=recv_sems.at[kind],
+            device_id={"cell": lax.rem(me + 1, n_cell)},
             device_id_type=MESH,
         )
 
-    def each(action):
-        def step(j, carry):
-            action(j)
-            return carry
-
-        lax.fori_loop(1, n_cell, step, 0)
-
-    def arrival(kind, source, target, j):
-        origin = lax.rem(me + n_cell - j, n_cell)
-        return pltpu.make_async_remote_copy(
-            src_ref=source if kind == 3 else source.at[origin],
-            dst_ref=target.at[origin],
-            send_sem=send_sems.at[kind, j],
-            recv_sem=recv_sems.at[kind, j],
-            device_id={"cell": origin},
-            device_id_type=MESH,
-        )
-
-    each(lambda j: copy(0, send_meta, got_meta, j).start())
-    each(lambda j: copy(1, send_a, got_a, j).start())
+    send(0, send_meta, got_meta)
+    send(1, send_a, got_a)
     got_meta[me] = send_meta[me]
     got_a[me] = send_a[me]
-    each(lambda j: arrival(0, send_meta, got_meta, j).wait_recv())
-    fetch = pltpu.make_async_copy(got_meta, meta_here, here_sem)
+    every(0, got_meta).wait_recv()
+    whole = got_meta[0]
+    for q in range(1, n_cell):
+        whole = whole + got_meta[q]
+    merged[...] = whole[0:1]
+    meta[...] = whole[0:1]
+    fetch = pltpu.make_async_copy(merged, meta_here, here_sems.at[0])
     fetch.start()
     fetch.wait()
     for q in range(n_cell):
         for k in range(2):
-            send_b[q, k] = block[meta_here[q, 0, k]]
-    each(lambda j: copy(2, send_b, got_b, j).start())
+            send_b[q, k] = sent[meta_here[0, 4 * q + k]]
+    send(2, send_b, got_b)
     got_b[me] = send_b[me]
 
     acc[...] = jnp.zeros_like(acc)
@@ -157,9 +181,9 @@
         moments = jnp.where(sub == d, row * scale, moments)
     mom_out[...] = jnp.zeros_like(mom_out)
     mom_out[:, 0:terms] = moments
-    each(lambda j: copy(3, mom_out, mom_in, j).start())
+    send(3, mom_out, mom_in)
     mom_in[me] = mom_out[...]
-    each(lambda j: arrival(3, mom_out, mom_in, j).wait_recv())
+    every(3, mom_in).wait_recv()
     gathered = mom_in[0]
     for q in range(1, n_cell):
         gathered = gathered + mom_in[q]
@@ -183,26 +207,28 @@
     lower = jnp.where(slab == 0, 0.0, beside[0])
     upper = jnp.where(slab == n_slab - 1, 0.0, beside[1])
     coef = jnp.zeros((8, NT), f32)
+    loads[3].wait()
     for k, source in enumerate((total[...], lower, upper)):
         coef = coef + lax.dot_general(
             source[:, 0:NT], translate[k], NT_DIMS, precision=highest, preferred_element_type=f32
         )
-    local[...] = jnp.zeros_like(local)
-    local[:, 0:NT] = coef
-
-    each(lambda j: arrival(1, send_a, got_a, j).wait_recv())
-    each(lambda j: arrival(2, send_b, got_b, j).wait_recv())
-    each(lambda j: copy(0, send_meta, got_meta, j).wait_send())
-    each(lambda j: copy(1, send_a, got_a, j).wait_send())
-    each(lambda j: copy(2, send_b, got_b, j).wait_send())
-    each(lambda j: copy(3, mom_out, mom_in, j).wait_send())
+    local[...] = coef[0:3]
+
+    every(1, got_a).wait_recv()
+    every(2, got_b).wait_recv()
+    every(0, got_meta).wait_send()
+    every(1, got_a).wait_send()
+    every(2, got_b).wait_send()
+    every(3, mom_in).wait_send()
 
 
 def field_kernel(
-    meta, owner, live, local, block, got_a, got_b, points, upsample,
+    meta, owner, live, local, block, got_a, got_b, points, upsample_hbm,
     out,
-    cell_list, packed, spread, up_high, up_low, left, right, table, columns,
+    cell_list, upsample, packed, spread, up_high, up_low, left, right, table, columns, load_sem,
 ):
+    load = pltpu.make_async_copy(upsample_hbm, upsample, load_sem)
+    load.start()
     cells, count, up_count = out.shape[1], out.shape[2], upsample.shape[1]
     n_cell = got_a.shape[0]
 
@@ -232,26 +258,43 @@
 
     lax.fori_loop(0, cells // 16, far_rows, 0)
 
+    row8 = lax.broadcasted_iota(jnp.int32, (8, 128), 0)
+    lane8 = lax.broadcasted_iota(jnp.int32, (8, 128), 1)
+
+    def take(n, data):
+        last = jnp.zeros((8, 128), f32)
+        for k in range(2):
+            first, second = data[3 + 4 * k : 4 + 4 * k, 0:128], data[3 + 4 * k : 4 + 4 * k, 128:256]
+            last = jnp.where(row8 == 4 * k, first, last)
+            last = jnp.where(row8 == 4 * k + 1, pltpu.roll(first, 64, 1), last)
+            last = jnp.where(row8 == 4 * k + 2, second, last)
+        for d in range(3):
+            at_centre = (row8 == d) & (lane8 == count - 256)
+            last = jnp.where(at_centre, data[3:4, 192 + d : 193 + d], last)
+        packed[n, :, 0:256] = data
+        packed[n, :, 256:384] = last
+
     def list_slot(s, n):
         q, k = s // 2, lax.rem(s, 2)
-        flag, cell = live[0, q, k], owner[0, q, k]
+        flag = live[0, k, q]
 
         @pl.when(flag > 0)
         def _():
-            cell_list[n] = cell
-            packed[n] = got_b[q, k]
+            cell_list[n] = owner[0, k, q]
+            take(n, got_b[q, k])
 
         n = n + jnp.where(flag > 0, 1, 0)
-        flag_in, cell_in = meta[q, 0, 2 + k], meta[q, 0, k]
+        flag_in = meta[0, 4 * q + 2 + k]
 
         @pl.when(flag_in > 0)
         def _():
-            cell_list[n] = cell_in
-            packed[n] = got_a[q, k]
+            cell_list[n] = meta[0, 4 * q + k]
+            take(n, got_a[q, k])
 
         return n + jnp.where(flag_in > 0, 1, 0)
 
     units = lax.fori_loop(0, 2 * n_cell, list_slot, jnp.int32(0))
+    load.wait()
 
     up_high[...] = jnp.zeros_like(up_high)
     up_low[...] = jnp.zeros_like(up_low)
@@ -349,48 +392,58 @@
     n_cell = owner_cell.shape[1]
     vmem = pl.BlockSpec(memory_space=pltpu.VMEM)
     smem = pl.BlockSpec(memory_space=pltpu.SMEM)
-    slots = (n_cell, 2, 8, LANES)
-    got_a, got_b, got_meta, block, points, local = pl.pallas_call(
+    hbm = pl.BlockSpec(memory_space=pltpu.HBM)
+    got = (n_cell, 2, 8, 256)
+    owner, peer, live = (jnp.transpose(v, (0, 2, 1)) for v in (owner_cell, peer_cell, live))
+    got_a, got_b, meta, block, points, local = pl.pallas_call(
         exchange_kernel,
         out_shape=(
-            jax.ShapeDtypeStruct(slots, f32),
-            jax.ShapeDtypeStruct(slots, f32),
-            jax.ShapeDtypeStruct((n_cell, 8, 128), jnp.int32),
+            jax.ShapeDtypeStruct(got, f32),
+            jax.ShapeDtypeStruct(got, f32),
+            jax.ShapeDtypeStruct((1, 128), jnp.int32),
             jax.ShapeDtypeStruct((cells, 8, LANES), f32),
             jax.ShapeDtypeStruct((3, cells, LANES), f32),
-            jax.ShapeDtypeStruct((8, 256), f32),
+            jax.ShapeDtypeStruct((3, NT), f32),
         ),
-        in_specs=[smem] * 3 + [vmem] * 4,
+        in_specs=[smem] * 3 + [hbm] * 4,
         out_specs=(vmem,) * 6,
         scratch_shapes=[
-            pltpu.VMEM(slots, f32),
-            pltpu.VMEM(slots, f32),
+            pltpu.VMEM(centers.shape, f32),
+            pltpu.VMEM(offsets.shape, f32),
+            pltpu.VMEM(forces.shape, f32),
+            pltpu.VMEM(translate.shape, f32),
+            pltpu.VMEM((cells, 8, 256), f32),
+            pltpu.VMEM(got, f32),
+            pltpu.VMEM(got, f32),
             pltpu.VMEM((n_cell, 8, 128), jnp.int32),
-            pltpu.SMEM((n_cell, 8, 128), jnp.int32),
+            pltpu.VMEM((n_cell, 8, 128), jnp.int32),
+            pltpu.VMEM((1, 128), jnp.int32),
+            pltpu.SMEM((1, 128), jnp.int32),
             pltpu.VMEM((8, 256), f32),
             pltpu.VMEM((n_cell, 8, 256), f32),
             pltpu.VMEM((8, 256), f32),
             pltpu.VMEM((2, 8, 256), f32),
             pltpu.VMEM((6, cells, LANES), f32),
             pltpu.VMEM((3, 168, 8, 128), f32),
-            pltpu.SemaphoreType.DMA((4, n_cell)),
-            pltpu.SemaphoreType.DMA((4, n_cell)),
+            pltpu.SemaphoreType.DMA((4,)),
+            pltpu.SemaphoreType.DMA((4,)),
             pltpu.SemaphoreType.DMA((2,)),
             pltpu.SemaphoreType.DMA((2,)),
-            pltpu.SemaphoreType.DMA,
+            pltpu.SemaphoreType.DMA((4,)),
         ],
         compiler_params=pltpu.CompilerParams(
-            collective_id=0, has_side_effects=True, vmem_limit_bytes=32 * 1024 * 1024
+            collective_id=0, has_side_effects=True, vmem_limit_bytes=60 * 1024 * 1024
         ),
         name="exchange",
-    )(owner_cell, peer_cell, live, centers, offsets, forces, translate)
+    )(owner, peer, live, centers, offsets, forces, translate)
     return pl.pallas_call(
         field_kernel,
         out_shape=jax.ShapeDtypeStruct((3, cells, count), f32),
-        in_specs=[smem] * 4 + [vmem] * 5,
+        in_specs=[smem] * 4 + [vmem] * 4 + [hbm],
         out_specs=vmem,
         scratch_shapes=[
             pltpu.SMEM((cells,), jnp.int32),
+            pltpu.VMEM(upsample.shape, f32),
             pltpu.VMEM((cells, 8, LANES), f32),
             pltpu.VMEM((cells, 8, UP_LANES), f32),
             pltpu.VMEM((count, UP_LANES), bf16),
@@ -399,10 +452,11 @@
             pltpu.VMEM((cells, 64, UP_LANES), bf16),
             pltpu.VMEM((cells, 8, UP_LANES), f32),
             pltpu.VMEM((LANES, 128), f32),
+            pltpu.SemaphoreType.DMA,
         ],
-        compiler_params=pltpu.CompilerParams(vmem_limit_bytes=50 * 1024 * 1024),
+        compiler_params=pltpu.CompilerParams(vmem_limit_bytes=61 * 1024 * 1024),
         name="field",
-    )(got_meta, owner_cell, live, local, block, got_a, got_b, points, upsample)
+    )(meta, owner, live, local, block, got_a, got_b, points, upsample)
 
 
 def solution(mesh):

time: 109 us -> 102 us (0.936)
  the two profiles are of different devices: /device:TPU:129 before, /device:TPU:18 now
where the time goes in v1:
time: 102 us
  Pallas kernels  102 us (100%)
    pallas_call x1, Pallas kernels, on_device(): pl.pallas_call(field_kernel, out_shape=jax.ShapeDtypeStruct((3, cells, co...  75.5 us
    pallas_call x1, Pallas kernels, on_device(): pl.pallas_call(exchange_kernel, out_shape=(jax.ShapeDtypeStruct(got, f32)...  26.1 us

profile of v1, /device:TPU:18, one launch (start us, length us, event | category | flops | bytes accessed | tf_op | source)
XLA Modules:
  0.0 101.6 jit_solution(13819195099635167981)
XLA Ops:
  0.0 26.1 %exchange.1 = (f32[16,2,8,256]{3,2,1,0:T(8,128)}, f32[16,2,8,256]{3,2,1,0:T(8,128)}, s32[1,128]{1,0:T(1,128)}, f32[64,8,384]{2,1,0:T(8,128)}, f32[3,64,384]{2,1,0:T(8,128)}, /*index=5*/f32[3,165]{1,0:T(4,128)}) custom-call(s32[1,2,16]{2,1,0:T(2,128)} %bitcast.3, s32[1,2,16]{2,1,0:T(2,128)} %bitcast.7, s32[1,2,16]{2,1,0:T(2,128)} %bitcast.5, ...), custom_call_target="tpu_custom_call" | custom-call | tf_op jit(solution)/shard_map/exchange/pallas_call | solution.py:398
  26.1 75.5 %field.1 = f32[3,64,312]{2,1,0:T(8,128)} custom-call(s32[1,128]{1,0:T(1,128)} %get-tuple-element.11.meta, s32[1,2,16]{2,1,0:T(2,128)} %bitcast.4, s32[1,2,16]{2,1,0:T(2,128)} %bitcast.6, f32[3,165]{1,0:T(4,128)} %get-tuple-element.12.local, f32[64,8,384]{2,1,0:T(8,128)} %get-tuple-element.13.block, f32[16,2,8,256]{3,2,1,0:T(8,128)} %get-tuple-element.14.got_a, ...), custom_call_target="tpu_custom_call" | custom-call | tf_op jit(solution)/shard_map/field/pallas_call | solution.py:439

commit v2 on v1

--- a/solution.py
+++ b/solution.py
@@ -130,21 +130,6 @@
     send(1, send_a, got_a)
     got_meta[me] = send_meta[me]
     got_a[me] = send_a[me]
-    every(0, got_meta).wait_recv()
-    whole = got_meta[0]
-    for q in range(1, n_cell):
-        whole = whole + got_meta[q]
-    merged[...] = whole[0:1]
-    meta[...] = whole[0:1]
-    fetch = pltpu.make_async_copy(merged, meta_here, here_sems.at[0])
-    fetch.start()
-    fetch.wait()
-    for q in range(n_cell):
-        for k in range(2):
-            send_b[q, k] = sent[meta_here[0, 4 * q + k]]
-    send(2, send_b, got_b)
-    got_b[me] = send_b[me]
-
     acc[...] = jnp.zeros_like(acc)
 
     def moment_rows(i, carry):
@@ -182,6 +167,22 @@
     mom_out[...] = jnp.zeros_like(mom_out)
     mom_out[:, 0:terms] = moments
     send(3, mom_out, mom_in)
+
+    every(0, got_meta).wait_recv()
+    whole = got_meta[0]
+    for q in range(1, n_cell):
+        whole = whole + got_meta[q]
+    merged[...] = whole[0:1]
+    meta[...] = whole[0:1]
+    fetch = pltpu.make_async_copy(merged, meta_here, here_sems.at[0])
+    fetch.start()
+    fetch.wait()
+    for q in range(n_cell):
+        for k in range(2):
+            send_b[q, k] = sent[meta_here[0, 4 * q + k]]
+    send(2, send_b, got_b)
+    got_b[me] = send_b[me]
+
     mom_in[me] = mom_out[...]
     every(3, mom_in).wait_recv()
     gathered = mom_in[0]

time: 102 us -> 101 us (level)
  the two profiles are of different devices: /device:TPU:18 before, /device:TPU:186 now
where the time goes in v2:
time: 101 us
  Pallas kernels  101 us (100%)
    pallas_call x1, Pallas kernels, on_device(): pl.pallas_call(field_kernel, out_shape=jax.ShapeDtypeStruct((3, cells, co...  81.9 us
    pallas_call x1, Pallas kernels, on_device(): pl.pallas_call(exchange_kernel, out_shape=(jax.ShapeDtypeStruct(got, f32)...  18.7 us

profile of v2, /device:TPU:186, one launch (start us, length us, event | category | flops | bytes accessed | tf_op | source)
XLA Modules:
  0.0 100.6 jit_solution(7063909661206383221)
XLA Ops:
  0.0 18.7 %exchange.1 = (f32[16,2,8,256]{3,2,1,0:T(8,128)}, f32[16,2,8,256]{3,2,1,0:T(8,128)}, s32[1,128]{1,0:T(1,128)}, f32[64,8,384]{2,1,0:T(8,128)}, f32[3,64,384]{2,1,0:T(8,128)}, /*index=5*/f32[3,165]{1,0:T(4,128)}) custom-call(s32[1,2,16]{2,1,0:T(2,128)} %bitcast.3, s32[1,2,16]{2,1,0:T(2,128)} %bitcast.7, s32[1,2,16]{2,1,0:T(2,128)} %bitcast.5, ...), custom_call_target="tpu_custom_call" | custom-call | tf_op jit(solution)/shard_map/exchange/pallas_call | solution.py:399
  18.7 81.9 %field.1 = f32[3,64,312]{2,1,0:T(8,128)} custom-call(s32[1,128]{1,0:T(1,128)} %get-tuple-element.11.meta, s32[1,2,16]{2,1,0:T(2,128)} %bitcast.4, s32[1,2,16]{2,1,0:T(2,128)} %bitcast.6, f32[3,165]{1,0:T(4,128)} %get-tuple-element.12.local, f32[64,8,384]{2,1,0:T(8,128)} %get-tuple-element.13.block, f32[16,2,8,256]{3,2,1,0:T(8,128)} %get-tuple-element.14.got_a, ...), custom_call_target="tpu_custom_call" | custom-call | tf_op jit(solution)/shard_map/field/pallas_call | solution.py:440

commit v3 on v2

--- a/solution.py
+++ b/solution.py
@@ -31,7 +31,7 @@
 
 def exchange_kernel(
     owner, peer, live, centers_hbm, offsets_hbm, forces_hbm, translate_hbm,
-    got_a, got_b, meta, block, points, local,
+    got, meta, block, points, local,
     centers, offsets, forces, translate, sent, send_a, send_b, send_meta, got_meta, merged, meta_here,
     mom_out, mom_in, total, beside, padded, acc,
     send_sems, recv_sems, side_send, side_recv, here_sems,
@@ -44,6 +44,7 @@
     below = lax.rem(slab + n_slab - 1, n_slab)
     cells, count = offsets.shape[1], offsets.shape[2]
 
+    got_a, got_b = got.at[0], got.at[1]
     barrier = pltpu.get_barrier_semaphore()
     pairs = ((centers_hbm, centers), (offsets_hbm, offsets), (forces_hbm, forces), (translate_hbm, translate))
     loads = [pltpu.make_async_copy(source, target, here_sems.at[k]) for k, (source, target) in enumerate(pairs)]
@@ -224,14 +225,14 @@
 
 
 def field_kernel(
-    meta, owner, live, local, block, got_a, got_b, points, upsample_hbm,
+    meta, owner, live, local, block, got, points, upsample_hbm,
     out,
-    cell_list, upsample, packed, spread, up_high, up_low, left, right, table, columns, load_sem,
+    cell_list, source_list, upsample, packed, spread, up_high, up_low, left, right, table, columns, load_sem,
 ):
     load = pltpu.make_async_copy(upsample_hbm, upsample, load_sem)
     load.start()
     cells, count, up_count = out.shape[1], out.shape[2], upsample.shape[1]
-    n_cell = got_a.shape[0]
+    n_cell = owner.shape[2]
 
     def far_rows(i, carry):
         rows = pl.ds(pl.multiple_of(i * 16, 16), 16)
@@ -275,26 +276,24 @@
         packed[n, :, 0:256] = data
         packed[n, :, 256:384] = last
 
-    def list_slot(s, n):
-        q, k = s // 2, lax.rem(s, 2)
-        flag = live[0, k, q]
-
-        @pl.when(flag > 0)
-        def _():
+    def clear(n, carry):
+        cell_list[n] = 0
+        source_list[n] = 0
+        return carry
+
+    lax.fori_loop(0, cells, clear, 0)
+
+    def list_slot(q, n):
+        for k in range(2):
             cell_list[n] = owner[0, k, q]
-            take(n, got_b[q, k])
-
-        n = n + jnp.where(flag > 0, 1, 0)
-        flag_in = meta[0, 4 * q + 2 + k]
-
-        @pl.when(flag_in > 0)
-        def _():
+            source_list[n] = 2 * n_cell + 2 * q + k
+            n = n + live[0, k, q]
             cell_list[n] = meta[0, 4 * q + k]
-            take(n, got_a[q, k])
-
-        return n + jnp.where(flag_in > 0, 1, 0)
-
-    units = lax.fori_loop(0, 2 * n_cell, list_slot, jnp.int32(0))
+            source_list[n] = 2 * q + k
+            n = n + meta[0, 4 * q + 2 + k]
+        return n
+
+    units = lax.fori_loop(0, n_cell, list_slot, jnp.int32(0))
     load.wait()
 
     up_high[...] = jnp.zeros_like(up_high)
@@ -306,6 +305,8 @@
 
     def spread_units(i, carry):
         rows = pl.ds(i * 16, 16)
+        for k in range(16):
+            take(i * 16 + k, got[source_list[i * 16 + k]])
         data = packed[rows].reshape(128, LANES)[:, 0:count]
         first = data.astype(bf16)
         second = (data - first.astype(f32)).astype(bf16)
@@ -319,7 +320,7 @@
 
     lax.fori_loop(0, (units + 15) // 16, spread_units, 0)
 
-    def build(u, carry):
+    def build(u):
         cell = cell_list[u]
         target = block[cell]
         row = lax.broadcasted_iota(jnp.int32, (8, UP_LANES), 0)
@@ -348,9 +349,13 @@
         for k, rows in enumerate((order + [squares, zero], lower + [zero, zero])):
             turned = jnp.transpose(jnp.concatenate(rows, axis=0))
             left[u, k] = turned[0:count].astype(bf16)
-        return carry
-
-    lax.fori_loop(0, units, build, 0)
+
+    def build_two(i, carry):
+        build(2 * i)
+        build(2 * i + 1)
+        return carry
+
+    lax.fori_loop(0, (units + 1) // 2, build_two, 0)
 
     columns[...] = jnp.zeros_like(columns)
     step = 40
@@ -394,28 +399,27 @@
     vmem = pl.BlockSpec(memory_space=pltpu.VMEM)
     smem = pl.BlockSpec(memory_space=pltpu.SMEM)
     hbm = pl.BlockSpec(memory_space=pltpu.HBM)
-    got = (n_cell, 2, 8, 256)
+    slots = (n_cell, 2, 8, 256)
     owner, peer, live = (jnp.transpose(v, (0, 2, 1)) for v in (owner_cell, peer_cell, live))
-    got_a, got_b, meta, block, points, local = pl.pallas_call(
+    got, meta, block, points, local = pl.pallas_call(
         exchange_kernel,
         out_shape=(
-            jax.ShapeDtypeStruct(got, f32),
-            jax.ShapeDtypeStruct(got, f32),
+            jax.ShapeDtypeStruct((2,) + slots, f32),
             jax.ShapeDtypeStruct((1, 128), jnp.int32),
             jax.ShapeDtypeStruct((cells, 8, LANES), f32),
             jax.ShapeDtypeStruct((3, cells, LANES), f32),
             jax.ShapeDtypeStruct((3, NT), f32),
         ),
         in_specs=[smem] * 3 + [hbm] * 4,
-        out_specs=(vmem,) * 6,
+        out_specs=(vmem,) * 5,
         scratch_shapes=[
             pltpu.VMEM(centers.shape, f32),
             pltpu.VMEM(offsets.shape, f32),
             pltpu.VMEM(forces.shape, f32),
             pltpu.VMEM(translate.shape, f32),
             pltpu.VMEM((cells, 8, 256), f32),
-            pltpu.VMEM(got, f32),
-            pltpu.VMEM(got, f32),
+            pltpu.VMEM(slots, f32),
+            pltpu.VMEM(slots, f32),
             pltpu.VMEM((n_cell, 8, 128), jnp.int32),
             pltpu.VMEM((n_cell, 8, 128), jnp.int32),
             pltpu.VMEM((1, 128), jnp.int32),
@@ -440,10 +444,11 @@
     return pl.pallas_call(
         field_kernel,
         out_shape=jax.ShapeDtypeStruct((3, cells, count), f32),
-        in_specs=[smem] * 4 + [vmem] * 4 + [hbm],
+        in_specs=[smem] * 4 + [vmem] * 3 + [hbm],
         out_specs=vmem,
         scratch_shapes=[
-            pltpu.SMEM((cells,), jnp.int32),
+            pltpu.SMEM((cells + 1,), jnp.int32),
+            pltpu.SMEM((cells + 1,), jnp.int32),
             pltpu.VMEM(upsample.shape, f32),
             pltpu.VMEM((cells, 8, LANES), f32),
             pltpu.VMEM((cells, 8, UP_LANES), f32),
@@ -457,7 +462,7 @@
         ],
         compiler_params=pltpu.CompilerParams(vmem_limit_bytes=61 * 1024 * 1024),
         name="field",
-    )(meta, owner, live, local, block, got_a, got_b, points, upsample)
+    )(meta, owner, live, local, block, got.reshape(4 * n_cell, 8, 256), points, upsample)
 
 
 def solution(mesh):

time: 101 us -> 94.5 us (0.936)
  the two profiles are of different devices: /device:TPU:186 before, /device:TPU:9 now
where the time goes in v3:
time: 94.5 us; the launch traced here: 94.4 us
  Pallas kernels  94.4 us (100%)
    pallas_call x1, Pallas kernels, on_device(): pl.pallas_call(field_kernel, out_shape=jax.ShapeDtypeStruct((3, cells, co...  72.4 us
    pallas_call x1, Pallas kernels, on_device(): pl.pallas_call(exchange_kernel, out_shape=(jax.ShapeDtypeStruct((2,) + sl...  22 us

profile of v3, /device:TPU:9, one launch (start us, length us, event | category | flops | bytes accessed | tf_op | source)
XLA Modules:
  0.0 94.4 jit_solution(15204003744498221162)
XLA Ops:
  0.0 22.0 %exchange.1 = (f32[2,16,2,8,256]{4,3,2,1,0:T(8,128)}, s32[1,128]{1,0:T(1,128)}, f32[64,8,384]{2,1,0:T(8,128)}, f32[3,64,384]{2,1,0:T(8,128)}, f32[3,165]{1,0:T(4,128)}) custom-call(s32[1,2,16]{2,1,0:T(2,128)} %bitcast.5, s32[1,2,16]{2,1,0:T(2,128)} %bitcast.9, s32[1,2,16]{2,1,0:T(2,128)} %bitcast.7, f32[3,64]{1,0:T(4,128)} %centers_hbm.1, ...), custom_call_target="tpu_custom_call" | custom-call | tf_op jit(solution)/shard_map/exchange/pallas_call | solution.py:404
  22.0 72.4 %field.1 = f32[3,64,312]{2,1,0:T(8,128)} custom-call(s32[1,128]{1,0:T(1,128)} %get-tuple-element.10.meta, s32[1,2,16]{2,1,0:T(2,128)} %bitcast.6, s32[1,2,16]{2,1,0:T(2,128)} %bitcast.8, f32[3,165]{1,0:T(4,128)} %get-tuple-element.11.local, f32[64,8,384]{2,1,0:T(8,128)} %get-tuple-element.12.block, f32[64,8,256]{2,1,0:T(8,128)} %bitcast.4, ...), custom_call_target="tpu_custom_call" | custom-call | tf_op jit(solution)/shard_map/field/pallas_call | solution.py:444
